TPU v7x, 32 devices: a whole 2x2x4 slice. The times are simulated.
32 devices in a mesh: bed: 8 (over y, x, core), layer: 4 (over z).
Axes of the slice: x: 2, y: 2, z: 4, core: 2. Of those that a mesh axis runs over, the one named last changes fastest.
Arguments:
- concentration: float32 [8, 1024, 4096], P('layer', 'bed'), may hold values from 0.2 to 2
- east_velocity: bfloat16 [8, 1024, 4096], P('layer', 'bed'), may hold values from -3 to 3
- north_velocity: bfloat16 [8, 1024, 4096], P('layer', 'bed'), may hold values from -3 to 3
- settling: float32 [1024, 4096], P('bed'), may hold values from 0.02 to 0.15
- surface: float32 [1024, 4096], P('bed'), may hold values from 1.8 to 6
- bed_level: float32 [1024, 4096], P('bed'), may hold values from -1 to 1
- erosion: float32 [1024, 4096], P('bed'), may hold values from 0 to 0.08
- wet_mask: int32 [1024, 4096], P('bed'), may hold values 0 or 1
Outputs:
- new_concentration: float32 [8, 1024, 4096], P('layer', 'bed')
- new_bed: float32 [1024, 4096], P('bed')
Inputs may be any that keep to these rules, and one draw needn't show every extreme that they name: `wet_mask`: 1 marks a wet cell, 0 a dry one.
All inputs are finite; a program needn't handle non-finite values. No bound on the sum of `wet_mask` on one device may be relied on, other than what follows from the above.
Results may differ from a plain program's by a relative error of at most 0.0003.
Values sent between devices are 32-bit elements; how exact they have to be, the bound alone decides.
A program may use at most 128 MiB of HBM per device.

v0:
```python
import jax
import jax.numpy as jnp
from jax import lax
from jax.sharding import PartitionSpec as P

SWEEPS = 4
ADVECT_RATE = 0.1
FLUX_GAIN = 0.15
POROSITY_GAIN = 1.0 / 0.6
RELAX_RATE = 0.2
CRIT_SLOPE = 0.5
DEPTH_FLOOR = 1.0


def padded(block, sides, width):
    for axis, dim in sides:
        count = lax.axis_size(axis)
        forward = [(i, i + 1) for i in range(count - 1)]
        backward = [(target, source) for source, target in forward]
        low = lax.ppermute(
            lax.slice_in_dim(block, block.shape[dim] - width, None, axis=dim), axis, forward
        )
        high = lax.ppermute(lax.slice_in_dim(block, 0, width, axis=dim), axis, backward)
        block = jnp.concatenate([low, block, high], axis=dim)
    return block


def passed_along(block, axis, distance):
    devices = range(lax.axis_size(axis))
    route = [(i - distance, i) for i in devices if i - distance in devices]
    return lax.ppermute(block, axis, route)


def face_divergence(values, speeds, which_axis):
    length_here = values.shape[which_axis]
    left_val = lax.slice_in_dim(values, 0, length_here - 1, axis=which_axis)
    right_val = lax.slice_in_dim(values, 1, length_here, axis=which_axis)
    left_spd = lax.slice_in_dim(speeds, 0, length_here - 1, axis=which_axis)
    right_spd = lax.slice_in_dim(speeds, 1, length_here, axis=which_axis)
    face_speed = 0.5 * (left_spd + right_spd)
    face_flux = jnp.maximum(face_speed, 0.0) * left_val + jnp.minimum(face_speed, 0.0) * right_val
    return lax.slice_in_dim(face_flux, 1, length_here - 1, axis=which_axis) - lax.slice_in_dim(
        face_flux, 0, length_here - 2, axis=which_axis
    )


def slide_sweep(height, wetness):
    drop_x = height[:-1, :] - height[1:, :]
    move_x = (
        RELAX_RATE
        * (drop_x - jnp.clip(drop_x, -CRIT_SLOPE, CRIT_SLOPE))
        * wetness[:-1, :]
        * wetness[1:, :]
    )
    drop_y = height[:, :-1] - height[:, 1:]
    move_y = (
        RELAX_RATE
        * (drop_y - jnp.clip(drop_y, -CRIT_SLOPE, CRIT_SLOPE))
        * wetness[:, :-1]
        * wetness[:, 1:]
    )
    return (
        height[1:-1, 1:-1]
        - move_x[1:, 1:-1]
        + move_x[:-1, 1:-1]
        - move_y[1:-1, 1:]
        + move_y[1:-1, :-1]
    )


def edge_pair(field):
    return jnp.concatenate([field[:, :1], field[:, -1:]], 1)


def body(
    concentration, east_velocity, north_velocity, settling, surface, bed_level, erosion, wet_mask
):
    layers_here = concentration.shape[0]
    layer_count = layers_here * lax.axis_size("layer")
    layer_index = lax.axis_index("layer")
    water_depth = surface - bed_level
    layer_thick = water_depth / layer_count
    east_speed = east_velocity.astype(jnp.float32)
    north_speed = north_velocity.astype(jnp.float32)
    flux_east = east_speed * concentration * layer_thick
    flux_north = north_speed * concentration * layer_thick
    edges = jnp.stack([edge_pair(concentration), edge_pair(east_speed), edge_pair(flux_east)])
    rims = padded(edges, (("bed", 2),), 1)
    before = rims[:, :, :1]
    after = rims[:, :, 3:]
    conc_along = jnp.concatenate([before[0], concentration, after[0]], 1)
    speed_along = jnp.concatenate([before[1], east_speed, after[1]], 1)
    east_wide = jnp.concatenate([before[2], flux_east, after[2]], 1)
    upper_row = passed_along(concentration[0], "layer", -1)
    pad_y = ((0, 0), (0, 0), (1, 1))
    advect = face_divergence(conc_along, speed_along, 1) + face_divergence(
        jnp.pad(concentration, pad_y), jnp.pad(north_speed, pad_y), 2
    )
    bottom_flag = (layer_index == 0).astype(jnp.float32)
    falling = jnp.concatenate([concentration[1:], upper_row[None]], 0) * settling
    source = falling - settling * concentration
    source = source.at[0].add(bottom_flag * erosion)
    settled = concentration - ADVECT_RATE * advect + layer_count / water_depth * source
    north_wide = jnp.pad(flux_north, pad_y)
    spread = 0.5 * (
        east_wide[:, 2:, :] - east_wide[:, :-2, :] + north_wide[:, :, 2:] - north_wide[:, :, :-2]
    )
    bed_change = FLUX_GAIN * jnp.sum(spread, 0) - bottom_flag * settling * concentration[0]
    wet_float = wet_mask.astype(jnp.float32)
    rim_width, rounds = (1, SWEEPS)
    summed_flux = lax.psum(bed_change, "layer")
    height = bed_level - POROSITY_GAIN * wet_float * (summed_flux + erosion)
    side_pad = ((0, 0), (rim_width, rim_width))
    wet_wide = jnp.pad(padded(wet_float, (("bed", 0),), rim_width), side_pad)
    for round_index in range(rounds):
        height_wide = jnp.pad(padded(height, (("bed", 0),), rim_width), side_pad)
        wetness = wet_wide
        height_wide = slide_sweep(height_wide, wetness)
        wetness = wetness[1:-1, 1:-1]
        height = height_wide
    new_depth = jnp.maximum(surface - height, DEPTH_FLOOR)
    return (settled * (water_depth / new_depth), height)


def solution(mesh):
    in_specs = (
        P("layer", "bed", None),
        P("layer", "bed", None),
        P("layer", "bed", None),
        P("bed", None),
        P("bed", None),
        P("bed", None),
        P("bed", None),
        P("bed", None),
    )
    out_specs = (P("layer", "bed", None), P("bed", None))
    return jax.shard_map(body, mesh=mesh, in_specs=in_specs, out_specs=out_specs, check_vma=False)
```

profile of v0, /device:TPU:4, one launch (start us, length us, event | category | flops | bytes accessed | tf_op | source)
XLA Modules:
  0.0 256.3 jit_solution(9465956623220491633)
XLA Ops:
  7.2 0.0 all-reduce.10.cloned.1.call-start
  7.2 0.0 copy-start
  7.2 0.0 copy-start.16
  7.2 2.7 %fusion.39 = (f32[1,128,4096]{2,1,0:T(8,128)S(1)}, f32[128,4096]{1,0:T(8,128)S(1)}) fusion(f32[2,128,4096]{2,1,0:T(8,128)} %param.10), kind=kLoop, calls=%fused_computation.111 | loop fusion | bytes 8388608 | tf_op jit(solution)/shard_map/slice | solution.py:100
  9.9 1.6 collective-permute-start.2
  11.6 0.1 maximum_bitcast_fusion
  11.7 0.2 copy-done.16
  11.9 3.4 %broadcast_divide_fusion = (f32[128,4096]{1,0:T(8,128)}, f32[128,4096]{1,0:T(8,128)S(1)}) fusion(f32[128,4096]{1,0:T(8,128)} %param.14, f32[128,4096]{1,0:T(8,128)S(1)} %copy-done.16), kind=kLoop, calls=%fused_computation.99 | loop fusion | flops 1048576 | bytes 8388608 | tf_op jit(solution)/shard_map/div | solution.py:103
  15.3 1.3 copy-done.5
  16.6 0.2 broadcast_multiply_fusion
  16.8 42.6 %collective-permute-done.2 = f32[128,4096]{1,0:T(8,128)S(1)} collective-permute-done((f32[128,4096]{1,0:T(8,128)S(1)}, f32[128,4096]{1,0:T(8,128)S(1)}, u32[]{:S(2)}, u32[]{:S(2)}) %collective-permute-start.2) | collective-permute-done | bytes 2097184 | tf_op jit(solution)/shard_map/ppermute | solution.py:31
  59.5 4.4 %multiply_multiply_fusion = (f32[2,128,4096]{2,1,0:T(8,128)}, f32[2,128,4096]{2,1,0:T(8,128)S(1)}, f32[2,128,4096]{2,1,0:T(8,128)}) fusion(f32[2,128,4096]{2,1,0:T(8,128)S(1)} %copy-done, f32[128,4096]{1,0:T(8,128)S(1)} %broadcast_multiply_fusion, bf16[2,128,4096]{2,1,0:T(8,128)(2,1)S(1)} %copy-done.11, bf16[2,128,4096]{2,1,0:T(8,128)(2,1)S(1)} %copy-done.8, ...), kind=kLoop, calls=%fused_computation.22 | loop fusion | flops 10485760 | bytes 29360128 | tf_op jit(solution)/shard_map/mul | solution.py:86
  63.9 2.0 copy-done.6
  65.9 0.1 maximum_bitcast_fusion.2
  66.0 0.1 pad_maximum_fusion.2
  66.1 0.2 fusion.48
  66.3 1.9 collective-permute-start.1
  68.2 2.4 collective-permute-start
  70.7 4.4 %collective-permute-done = f32[3,2,1,4096]{3,2,1,0:T(1,128)S(1)} collective-permute-done((f32[3,2,1,4096]{3,2,1,0:T(1,128)S(1)}, f32[3,2,1,4096]{3,2,1,0:T(1,128)S(1)}, u32[]{:S(2)}, u32[]{:S(2)}) %collective-permute-start) | collective-permute-done | bytes 98336 | tf_op jit(solution)/shard_map/ppermute | solution.py:20
  75.1 0.0 copy-start.14
  75.1 8.3 %fusion.6 = f32[128,4096]{1,0:T(8,128)S(1)} fusion(f32[2,128,4096]{2,1,0:T(8,128)} %copy-done.6, f32[2,1,4096]{2,1,0:T(1,128)S(1)} %get-tuple-element.44, f32[2,1,4096]{2,1,0:T(1,128)S(1)} %get-tuple-element.41, f32[2,128,4096]{2,1,0:T(8,128)} %get-tuple-element.18), kind=kLoop, calls=%fused_computation.11 | loop fusion | flops 6815744 | bytes 10551296 | tf_op jit(solution)/shard_map/reduce_sum | solution.py:108
  83.4 1.8 multiply_subtract_fusion.1
  85.3 0.0 all-reduce.10.cloned.1.call-update
  85.3 0.0 copy-start.12
  85.3 1.9 convert_element_type.25
  87.2 1.4 copy-done.9
  88.6 1.9 collective-permute-start.5
  90.6 4.5 %collective-permute-start.6 = (f32[1,4096]{1,0:T(1,128)S(1)}, f32[1,4096]{1,0:T(1,128)S(1)}, u32[]{:S(2)}, u32[]{:S(2)}) collective-permute-start(f32[1,4096]{1,0:T(1,128)S(1)} %get-tuple-element.34), channel_id=1, source_target_pairs={{4,0},{8,4},{12,8},{16,12},{20,16},{24,20},{28,24},{5,1},{9,5},{13... | collective-permute-start | bytes 49160 | tf_op jit(solution)/shard_map/ppermute | solution.py:23
  95.1 2.5 convert_element_type.23
  97.6 73.6 %all-reduce.10.cloned.1.call-done = f32[128,4096]{1,0:T(8,128)} async-done(((f32[128,4096]{1,0:T(8,128)}), f32[128,4096]{1,0:T(8,128)}) %all-reduce.10.cloned.1.call-update) | async-done | bytes 2097168 | tf_op jit(solution)/shard_map/psum | solution.py:111
  171.2 4.2 %multiply_subtract_fusion = f32[128,4096]{1,0:T(8,128)S(1)} fusion(f32[128,4096]{1,0:T(8,128)} %param.15, f32[128,4096]{1,0:T(8,128)} %all-reduce.10.cloned.1.call-done, f32[128,4096]{1,0:T(8,128)} %param.16, s32[128,4096]{1,0:T(8,128)} %param.17), kind=kLoop, calls=%fused_computation.96 | loop fusion | flops 2621440 | bytes 10485760 | tf_op jit(solution)/shard_map/sub | solution.py:112
  175.5 1.9 collective-permute-start.3
  177.4 4.5 %collective-permute-start.4 = (f32[1,4096]{1,0:T(1,128)S(1)}, f32[1,4096]{1,0:T(1,128)S(1)}, u32[]{:S(2)}, u32[]{:S(2)}) collective-permute-start(f32[1,4096]{1,0:T(1,128)S(1)} %get-tuple-element.36), channel_id=1, source_target_pairs={{4,0},{8,4},{12,8},{16,12},{20,16},{24,20},{28,24},{5,1},{9,5},{13... | collective-permute-start | bytes 49160 | tf_op jit(solution)/shard_map/ppermute | solution.py:23
  182.0 0.7 select_maximum_fusion.6
  182.7 0.6 collective-permute-done.4
  183.4 0.7 select_maximum_fusion.8
  184.1 0.8 fusion.15
  184.9 1.3 fusion.18
  186.2 0.0 copy-start.2
  186.2 1.8 slice_add_fusion.6
  188.0 2.7 %collective-permute-start.7 = (f32[1,4096]{1,0:T(1,128)S(1)}, f32[1,4096]{1,0:T(1,128)S(1)}, u32[]{:S(2)}, u32[]{:S(2)}) collective-permute-start(f32[1,4096]{1,0:T(1,128)S(1)} %get-tuple-element.31), channel_id=1, source_target_pairs={{0,4},{4,8},{8,12},{12,16},{16,20},{20,24},{24,28},{1,5},{5,9},{9,... | collective-permute-start | bytes 49160 | tf_op jit(solution)/shard_map/ppermute | solution.py:20
  190.8 4.1 %collective-permute-start.8 = (f32[1,4096]{1,0:T(1,128)S(1)}, f32[1,4096]{1,0:T(1,128)S(1)}, u32[]{:S(2)}, u32[]{:S(2)}) collective-permute-start(f32[1,4096]{1,0:T(1,128)S(1)} %get-tuple-element.32), channel_id=1, source_target_pairs={{4,0},{8,4},{12,8},{16,12},{20,16},{24,20},{28,24},{5,1},{9,5},{13... | collective-permute-start | bytes 49160 | tf_op jit(solution)/shard_map/ppermute | solution.py:23
  194.9 2.4 multiply_add_fusion
  197.3 2.5 convert_element_type.22
  199.8 0.7 select_maximum_fusion.4
  200.5 0.8 fusion.21
  201.3 1.3 fusion.24
  202.6 1.8 slice_add_fusion.4
  204.4 2.4 collective-permute-start.10
  206.8 1.9 collective-permute-start.9
  208.8 0.6 fusion.38
  209.4 3.4 %collective-permute-done.9 = f32[1,4096]{1,0:T(1,128)S(1)} collective-permute-done((f32[1,4096]{1,0:T(1,128)S(1)}, f32[1,4096]{1,0:T(1,128)S(1)}, u32[]{:S(2)}, u32[]{:S(2)}) %collective-permute-start.9) | collective-permute-done | bytes 16416 | tf_op jit(solution)/shard_map/ppermute | solution.py:20
  212.8 0.7 select_maximum_fusion.2
  213.5 0.8 fusion.27
  214.3 1.3 fusion.30
  215.6 1.9 slice_add_fusion.2
  217.5 1.9 collective-permute-start.11
  219.4 4.8 %collective-permute-start.12 = (f32[1,4096]{1,0:T(1,128)S(1)}, f32[1,4096]{1,0:T(1,128)S(1)}, u32[]{:S(2)}, u32[]{:S(2)}) collective-permute-start(f32[1,4096]{1,0:T(1,128)S(1)} %get-tuple-element.28), channel_id=1, source_target_pairs={{4,0},{8,4},{12,8},{16,12},{20,16},{24,20},{28,24},{5,1},{9,5},{13... | collective-permute-start | bytes 49160 | tf_op jit(solution)/shard_map/ppermute | solution.py:23
  224.2 5.1 %fusion.1 = f32[2,129,4096]{2,1,0:T(8,128)S(1)} fusion(f32[2,128,4096]{2,1,0:T(8,128)S(1)} %copy-done.2, f32[2,1,4096]{2,1,0:T(1,128)S(1)} %get-tuple-element.45, f32[2,1,4096]{2,1,0:T(1,128)S(1)} %get-tuple-element.42, f32[2,1,4096]{2,1,0:T(1,128)S(1)} %get-tuple-element.43, f32[2,128,4096]{2,1,0:T(8,128)} %convert_element_type.22, ...), kind=kLoop, calls=%fused_computation.3 | loop fusion | flops 11624448 | bytes 12746752 | tf_op jit(solution)/shard_map/add | solution.py:41
  229.3 0.7 select_maximum_fusion
  230.0 2.2 fusion.33
  232.2 2.6 %fusion.36 = f32[130,4097]{1,0:T(8,128)} fusion(f32[130,4098]{1,0:T(8,128)S(1)} %select_maximum_fusion, f32[130,4098]{1,0:T(8,128)S(1)} %select_maximum_fusion.6), kind=kLoop, calls=%fused_computation.57 | loop fusion | flops 3195660 | bytes 10652200 | tf_op jit(solution)/shard_map/mul | solution.py:57
  234.9 9.2 %maximum_divide_fusion = (f32[128,4096]{1,0:T(8,128)}, f32[128,4096]{1,0:T(8,128)}) fusion(f32[128,4096]{1,0:T(8,128)} %copy-done.5, f32[128,4096]{1,0:T(8,128)} %param.14, f32[130,4097]{1,0:T(8,128)} %fusion.36, f32[129,4098]{1,0:T(8,128)} %fusion.33, f32[128,4096]{1,0:T(8,128)} %copy-done.4), kind=kLoop, calls=%fused_computation.95 | loop fusion | flops 3670016 | bytes 18874368 | tf_op jit(solution)/shard_map/div | solution.py:122
  244.0 5.4 %fusion.11 = f32[2,128,4096]{2,1,0:T(8,128)} fusion(f32[2,128,4096]{2,1,0:T(8,128)S(1)} %copy-done.2, f32[2,128,4097]{2,1,0:T(8,128)S(1)} %multiply_add_fusion, f32[2,129,4096]{2,1,0:T(8,128)S(1)} %fusion.1, f32[2,128,4096]{2,1,0:T(8,128)S(1)} %fusion.38, f32[128,4096]{1,0:T(8,128)} %get-tuple-element.16, f32[128,4096]{1,0:T(8,128)} %get-tuple-element.14), kind=kLoop, calls=%fused_computation.18 | loop fusion | flops 8388608 | bytes 33554432 | tf_op jit(solution)/shard_map/mul | solution.py:122
  (44 shorter events, 0.4 us)
Async XLA Ops:
  7.2 4.4 %copy-start.8 = (bf16[2,128,4096]{2,1,0:T(8,128)(2,1)S(1)}, bf16[2,128,4096]{2,1,0:T(8,128)(2,1)}, u32[]{:S(2)}) copy-start(bf16[2,128,4096]{2,1,0:T(8,128)(2,1)} %param.11) | copy-start | bytes 6291460
  7.2 164.1 %all-reduce.10.cloned.1.call-start = ((), (), s32[]{:S(2)}) async-start(), calls=%async_computation | async-start | bytes 4194304 | tf_op jit(solution)/shard_map/psum | solution.py:111
  7.2 4.3 %copy-start = (f32[2,128,4096]{2,1,0:T(8,128)S(1)}, f32[2,128,4096]{2,1,0:T(8,128)}, u32[]{:S(2)}) copy-start(f32[2,128,4096]{2,1,0:T(8,128)} %param.10) | copy-start | bytes 12582916
  7.2 4.7 %copy-start.16 = (f32[128,4096]{1,0:T(8,128)S(1)}, f32[128,4096]{1,0:T(8,128)}, u32[]{:S(2)}) copy-start(f32[128,4096]{1,0:T(8,128)} %param.15) | copy-start | bytes 6291460
  9.9 49.5 %collective-permute-start.2 = (f32[128,4096]{1,0:T(8,128)S(1)}, f32[128,4096]{1,0:T(8,128)S(1)}, u32[]{:S(2)}, u32[]{:S(2)}) collective-permute-start(f32[128,4096]{1,0:T(8,128)S(1)} %get-tuple-element.22), channel_id=1, source_target_pairs={{1,0},{2,1},{3,2},{5,4},{6,5},{7,6},{9,8},{10,9},{11,10},{13,12},{... | collective-permute-start | bytes 6291464 | tf_op jit(solution)/shard_map/ppermute | solution.py:31
  15.3 1.3 copy-start.5
  15.3 44.2 %copy-start.11 = (bf16[2,128,4096]{2,1,0:T(8,128)(2,1)S(1)}, bf16[2,128,4096]{2,1,0:T(8,128)(2,1)}, u32[]{:S(2)}) copy-start(bf16[2,128,4096]{2,1,0:T(8,128)(2,1)} %param.12) | copy-start | bytes 6291460
  15.3 44.2 %copy-start.13 = (f32[128,4096]{1,0:T(8,128)S(1)}, f32[128,4096]{1,0:T(8,128)}, u32[]{:S(2)}) copy-start(f32[128,4096]{1,0:T(8,128)} %param.13) | copy-start | bytes 6291460
  63.9 2.0 copy-start.6
  66.3 4.4 %collective-permute-start.1 = (f32[3,2,1,4096]{3,2,1,0:T(1,128)S(1)}, f32[3,2,1,4096]{3,2,1,0:T(1,128)S(1)}, u32[]{:S(2)}, u32[]{:S(2)}) collective-permute-start(f32[3,2,1,4096]{3,2,1,0:T(1,128)S(1)} %get-tuple-element.39), channel_id=1, source_target_pairs={{4,0},{8,4},{12,8},{16,12},{20,16},{24,20},{28,24},{5,1},{9,5},{13... | collective-permute-start | bytes 294920 | tf_op jit(solution)/shard_map/ppermute | solution.py:23
  68.2 6.8 %collective-permute-start = (f32[3,2,1,4096]{3,2,1,0:T(1,128)S(1)}, f32[3,2,1,4096]{3,2,1,0:T(1,128)S(1)}, u32[]{:S(2)}, u32[]{:S(2)}) collective-permute-start(f32[3,2,1,4096]{3,2,1,0:T(1,128)S(1)} %get-tuple-element.40), channel_id=1, source_target_pairs={{0,4},{4,8},{8,12},{12,16},{16,20},{20,24},{24,28},{1,5},{5,9},{9,... | collective-permute-start | bytes 294920 | tf_op jit(solution)/shard_map/ppermute | solution.py:20
  75.1 8.3 %copy-start.1 = (f32[2,128,4096]{2,1,0:T(8,128)S(1)}, f32[2,128,4096]{2,1,0:T(8,128)}, u32[]{:S(2)}) copy-start(f32[2,128,4096]{2,1,0:T(8,128)} %param.10) | copy-start | bytes 12582916
  75.1 8.3 %copy-start.14 = (f32[128,4096]{1,0:T(8,128)S(1)}, f32[128,4096]{1,0:T(8,128)}, u32[]{:S(2)}) copy-start(f32[128,4096]{1,0:T(8,128)} %param.13) | copy-start | bytes 6291460
  85.3 9.8 %copy-start.12 = (bf16[2,128,4096]{2,1,0:T(8,128)(2,1)S(1)}, bf16[2,128,4096]{2,1,0:T(8,128)(2,1)}, u32[]{:S(2)}) copy-start(bf16[2,128,4096]{2,1,0:T(8,128)(2,1)} %param.12) | copy-start | bytes 6291460
  87.2 1.4 copy-start.9
  88.6 93.3 %collective-permute-start.5 = (f32[1,4096]{1,0:T(1,128)S(1)}, f32[1,4096]{1,0:T(1,128)S(1)}, u32[]{:S(2)}, u32[]{:S(2)}) collective-permute-start(f32[1,4096]{1,0:T(1,128)S(1)} %get-tuple-element.33), channel_id=1, source_target_pairs={{0,4},{4,8},{8,12},{12,16},{16,20},{20,24},{24,28},{1,5},{5,9},{9,... | collective-permute-start | bytes 49160 | tf_op jit(solution)/shard_map/ppermute | solution.py:20
  90.6 91.4 %collective-permute-start.6 = (f32[1,4096]{1,0:T(1,128)S(1)}, f32[1,4096]{1,0:T(1,128)S(1)}, u32[]{:S(2)}, u32[]{:S(2)}) collective-permute-start(f32[1,4096]{1,0:T(1,128)S(1)} %get-tuple-element.34), channel_id=1, source_target_pairs={{4,0},{8,4},{12,8},{16,12},{20,16},{24,20},{28,24},{5,1},{9,5},{13... | collective-permute-start | bytes 49160 | tf_op jit(solution)/shard_map/ppermute | solution.py:23
  171.2 10.7 %copy-start.10 = (f32[128,4096]{1,0:T(8,128)S(1)}, f32[128,4096]{1,0:T(8,128)}, u32[]{:S(2)}) copy-start(f32[128,4096]{1,0:T(8,128)} %copy-done.9) | copy-start | bytes 6291460
  175.5 7.2 %collective-permute-start.3 = (f32[1,4096]{1,0:T(1,128)S(1)}, f32[1,4096]{1,0:T(1,128)S(1)}, u32[]{:S(2)}, u32[]{:S(2)}) collective-permute-start(f32[1,4096]{1,0:T(1,128)S(1)} %get-tuple-element.35), channel_id=1, source_target_pairs={{0,4},{4,8},{8,12},{12,16},{16,20},{20,24},{24,28},{1,5},{5,9},{9,... | collective-permute-start | bytes 49160 | tf_op jit(solution)/shard_map/ppermute | solution.py:20
  177.4 6.0 %collective-permute-start.4 = (f32[1,4096]{1,0:T(1,128)S(1)}, f32[1,4096]{1,0:T(1,128)S(1)}, u32[]{:S(2)}, u32[]{:S(2)}) collective-permute-start(f32[1,4096]{1,0:T(1,128)S(1)} %get-tuple-element.36), channel_id=1, source_target_pairs={{4,0},{8,4},{12,8},{16,12},{20,16},{24,20},{28,24},{5,1},{9,5},{13... | collective-permute-start | bytes 49160 | tf_op jit(solution)/shard_map/ppermute | solution.py:23
  186.2 8.7 %copy-start.2 = (f32[2,128,4096]{2,1,0:T(8,128)S(1)}, f32[2,128,4096]{2,1,0:T(8,128)}, u32[]{:S(2)}) copy-start(f32[2,128,4096]{2,1,0:T(8,128)} %param.10) | copy-start | bytes 12582916
  186.2 8.7 %copy-start.7 = (f32[2,128,4096]{2,1,0:T(8,128)S(1)}, f32[2,128,4096]{2,1,0:T(8,128)}, u32[]{:S(2)}) copy-start(f32[2,128,4096]{2,1,0:T(8,128)} %convert_element_type.23) | copy-start | bytes 12582916
  188.0 11.7 %collective-permute-start.7 = (f32[1,4096]{1,0:T(1,128)S(1)}, f32[1,4096]{1,0:T(1,128)S(1)}, u32[]{:S(2)}, u32[]{:S(2)}) collective-permute-start(f32[1,4096]{1,0:T(1,128)S(1)} %get-tuple-element.31), channel_id=1, source_target_pairs={{0,4},{4,8},{8,12},{12,16},{16,20},{20,24},{24,28},{1,5},{5,9},{9,... | collective-permute-start | bytes 49160 | tf_op jit(solution)/shard_map/ppermute | solution.py:20
  190.8 9.0 %collective-permute-start.8 = (f32[1,4096]{1,0:T(1,128)S(1)}, f32[1,4096]{1,0:T(1,128)S(1)}, u32[]{:S(2)}, u32[]{:S(2)}) collective-permute-start(f32[1,4096]{1,0:T(1,128)S(1)} %get-tuple-element.32), channel_id=1, source_target_pairs={{4,0},{8,4},{12,8},{16,12},{20,16},{24,20},{28,24},{5,1},{9,5},{13... | collective-permute-start | bytes 49160 | tf_op jit(solution)/shard_map/ppermute | solution.py:23
  202.6 6.2 %copy-start.3 = (f32[2,128,4096]{2,1,0:T(8,128)S(1)}, f32[2,128,4096]{2,1,0:T(8,128)}, u32[]{:S(2)}) copy-start(f32[2,128,4096]{2,1,0:T(8,128)} %get-tuple-element.20) | copy-start | bytes 12582916
  202.6 6.2 %copy-start.15 = (f32[128,4096]{1,0:T(8,128)S(1)}, f32[128,4096]{1,0:T(8,128)}, u32[]{:S(2)}) copy-start(f32[128,4096]{1,0:T(8,128)} %param.16) | copy-start | bytes 6291460
  204.4 5.0 %collective-permute-start.10 = (f32[1,4096]{1,0:T(1,128)S(1)}, f32[1,4096]{1,0:T(1,128)S(1)}, u32[]{:S(2)}, u32[]{:S(2)}) collective-permute-start(f32[1,4096]{1,0:T(1,128)S(1)} %get-tuple-element.30), channel_id=1, source_target_pairs={{4,0},{8,4},{12,8},{16,12},{20,16},{24,20},{28,24},{5,1},{9,5},{13... | collective-permute-start | bytes 49160 | tf_op jit(solution)/shard_map/ppermute | solution.py:23
  206.8 6.0 %collective-permute-start.9 = (f32[1,4096]{1,0:T(1,128)S(1)}, f32[1,4096]{1,0:T(1,128)S(1)}, u32[]{:S(2)}, u32[]{:S(2)}) collective-permute-start(f32[1,4096]{1,0:T(1,128)S(1)} %get-tuple-element.29), channel_id=1, source_target_pairs={{0,4},{4,8},{8,12},{12,16},{16,20},{20,24},{24,28},{1,5},{5,9},{9,... | collective-permute-start | bytes 49160 | tf_op jit(solution)/shard_map/ppermute | solution.py:20
  217.4 11.9 %copy-start.4 = (f32[128,4096]{1,0:T(8,128)}, f32[128,4096]{1,0:T(8,128)S(1)}, u32[]{:S(2)}) copy-start(f32[128,4096]{1,0:T(8,128)S(1)} %slice_add_fusion.2) | copy-start | bytes 6291460
  217.5 11.8 %collective-permute-start.11 = (f32[1,4096]{1,0:T(1,128)S(1)}, f32[1,4096]{1,0:T(1,128)S(1)}, u32[]{:S(2)}, u32[]{:S(2)}) collective-permute-start(f32[1,4096]{1,0:T(1,128)S(1)} %get-tuple-element.27), channel_id=1, source_target_pairs={{0,4},{4,8},{8,12},{12,16},{16,20},{20,24},{24,28},{1,5},{5,9},{9,... | collective-permute-start | bytes 49160 | tf_op jit(solution)/shard_map/ppermute | solution.py:20
  219.4 9.9 %collective-permute-start.12 = (f32[1,4096]{1,0:T(1,128)S(1)}, f32[1,4096]{1,0:T(1,128)S(1)}, u32[]{:S(2)}, u32[]{:S(2)}) collective-permute-start(f32[1,4096]{1,0:T(1,128)S(1)} %get-tuple-element.28), channel_id=1, source_target_pairs={{4,0},{8,4},{12,8},{16,12},{20,16},{24,20},{28,24},{5,1},{9,5},{13... | collective-permute-start | bytes 49160 | tf_op jit(solution)/shard_map/ppermute | solution.py:23
Sparse Core Ops, SparseCore 0:
  85.4 85.7 all-reduce.9
where the time goes:
time: 257 us; the launch traced here: 256 us
  waiting for transfers between devices  125 us (49%)
  other arithmetic  72.3 us (28%)
  starting transfers between devices  36.6 us (14%)
  between operations  14.6 us (6%)
  local copies, waits for them, and re-layouts  8.08 us (3%)
    psum x1, waiting for transfers between devices, body(): summed_flux = lax.psum(bed_change, 'layer')  73.6 us
    ppermute x1, waiting for transfers between devices, passed_along(): return lax.ppermute(block, axis, route)  42.6 us
    ppermute x6, starting transfers between devices, padded(): lax.ppermute(lax.slice_in_dim(block, 0, width, axis=dim), axis, backward)  22.2 us
    ppermute x6, starting transfers between devices, padded(): lax.ppermute(lax.slice_in_dim(block, block.shape[dim] - width, None, axis...  12.8 us
    div x1, other arithmetic, body(): return (settled * (water_depth / new_depth), height)  9.16 us
    reduce_sum x1, other arithmetic, body(): jnp.sum(spread, 0)  8.31 us
    ppermute x6, waiting for transfers between devices, padded(): lax.ppermute(lax.slice_in_dim(block, block.shape[dim] - width, None, axis...  7.76 us
    add x2, other arithmetic, face_divergence(): jnp.maximum(face_speed, 0.0) * left_val  7.51 us
  transfers between devices with their start and end apart: 14, of which 5 were waited for; matrix products, arithmetic and copies ran while one was open for 9% of the time, Pallas kernels for 0%

commit v1 on v0

--- a/solution.py
+++ b/solution.py
@@ -75,6 +75,10 @@
 def body(
     concentration, east_velocity, north_velocity, settling, surface, bed_level, erosion, wet_mask
 ):
+
+    def produce_weights(mine):
+        return lax.all_gather(mine, axis_name="layer").sum(axis=0)
+
     layers_here = concentration.shape[0]
     layer_count = layers_here * lax.axis_size("layer")
     layer_index = lax.axis_index("layer")
@@ -108,7 +112,7 @@
     bed_change = FLUX_GAIN * jnp.sum(spread, 0) - bottom_flag * settling * concentration[0]
     wet_float = wet_mask.astype(jnp.float32)
     rim_width, rounds = (1, SWEEPS)
-    summed_flux = lax.psum(bed_change, "layer")
+    summed_flux = produce_weights(bed_change)
     height = bed_level - POROSITY_GAIN * wet_float * (summed_flux + erosion)
     side_pad = ((0, 0), (rim_width, rim_width))
     wet_wide = jnp.pad(padded(wet_float, (("bed", 0),), rim_width), side_pad)

time: 257 us -> 325 us (1.26)
  waiting for transfers between devices: 125 us -> 188 us
  other arithmetic: 72.3 us -> 78.1 us
    all_gather x0 -> x1, waiting for transfers between devices: none -> 137 us  [produce_weights(): return lax.all_gather(mine, axis_name='layer').sum(axis=0)]
    psum x1 -> x0, waiting for transfers between devices: 73.6 us -> none  [body(): summed_flux = lax.psum(bed_change, 'layer')]
    reduce_sum x0 -> x1, other arithmetic: none -> 5.54 us  [produce_weights(): return lax.all_gather(mine, axis_name='layer').sum(axis=0)]
where the time goes in v1:
time: 325 us
  waiting for transfers between devices  188 us (58%)
  other arithmetic  78.1 us (24%)
  starting transfers between devices  36.6 us (11%)
  between operations  14.6 us (4%)
  local copies, waits for them, and re-layouts  7.94 us (2%)
    all_gather x1, waiting for transfers between devices, produce_weights(): return lax.all_gather(mine, axis_name='layer').sum(axis=0)  137 us
    ppermute x1, waiting for transfers between devices, passed_along(): return lax.ppermute(block, axis, route)  42.7 us
    ppermute x6, starting transfers between devices, padded(): lax.ppermute(lax.slice_in_dim(block, 0, width, axis=dim), axis, backward)  22 us
    ppermute x6, starting transfers between devices, padded(): lax.ppermute(lax.slice_in_dim(block, block.shape[dim] - width, None, axis...  13.1 us
    div x1, other arithmetic, body(): return (settled * (water_depth / new_depth), height)  9.16 us
    reduce_sum x1, other arithmetic, body(): jnp.sum(spread, 0)  8.48 us
    add x2, other arithmetic, face_divergence(): jnp.maximum(face_speed, 0.0) * left_val  7.76 us
    ppermute x6, waiting for transfers between devices, padded(): lax.ppermute(lax.slice_in_dim(block, block.shape[dim] - width, None, axis...  7.54 us
  transfers between devices with their start and end apart: 14, of which 5 were waited for; matrix products, arithmetic and copies ran while one was open for 9% of the time, Pallas kernels for 0%

profile of v1, /device:TPU:4, one launch (start us, length us, event | category | flops | bytes accessed | tf_op | source)
XLA Modules:
  0.0 324.8 jit_solution(6414915394457341020)
XLA Ops:
  7.2 0.0 all-gather.3.cloned.1.call-start
  7.2 0.0 copy-start
  7.2 2.7 fusion.39
  9.9 1.6 collective-permute-start.2
  11.6 0.1 maximum_bitcast_fusion
  11.7 0.2 copy-done.16
  11.9 3.3 %broadcast_divide_fusion = (f32[128,4096]{1,0:T(8,128)}, f32[128,4096]{1,0:T(8,128)S(1)}) fusion(f32[128,4096]{1,0:T(8,128)} %param.14, f32[128,4096]{1,0:T(8,128)S(1)} %copy-done.16), kind=kLoop, calls=%fused_computation.99 | loop fusion | flops 1048576 | bytes 8388608 | tf_op jit(solution)/shard_map/div | solution.py:107
  15.2 1.3 copy-done.5
  16.6 0.2 broadcast_multiply_fusion
  16.7 42.7 %collective-permute-done.2 = f32[128,4096]{1,0:T(8,128)S(1)} collective-permute-done((f32[128,4096]{1,0:T(8,128)S(1)}, f32[128,4096]{1,0:T(8,128)S(1)}, u32[]{:S(2)}, u32[]{:S(2)}) %collective-permute-start.2) | collective-permute-done | bytes 2097184 | tf_op jit(solution)/shard_map/ppermute | solution.py:31
  59.5 4.4 %multiply_multiply_fusion = (f32[2,128,4096]{2,1,0:T(8,128)}, f32[2,128,4096]{2,1,0:T(8,128)S(1)}, f32[2,128,4096]{2,1,0:T(8,128)}) fusion(f32[2,128,4096]{2,1,0:T(8,128)S(1)} %copy-done, f32[128,4096]{1,0:T(8,128)S(1)} %broadcast_multiply_fusion, bf16[2,128,4096]{2,1,0:T(8,128)(2,1)S(1)} %copy-done.11, bf16[2,128,4096]{2,1,0:T(8,128)(2,1)S(1)} %copy-done.8, ...), kind=kLoop, calls=%fused_computation.22 | loop fusion | flops 10485760 | bytes 29360128 | tf_op jit(solution)/shard_map/mul | solution.py:90
  63.8 2.0 copy-done.6
  65.8 0.1 maximum_bitcast_fusion.2
  65.9 0.1 pad_maximum_fusion.2
  66.0 0.2 fusion.48
  66.2 1.9 collective-permute-start.1
  68.1 2.4 collective-permute-start
  70.6 4.4 %collective-permute-done = f32[3,2,1,4096]{3,2,1,0:T(1,128)S(1)} collective-permute-done((f32[3,2,1,4096]{3,2,1,0:T(1,128)S(1)}, f32[3,2,1,4096]{3,2,1,0:T(1,128)S(1)}, u32[]{:S(2)}, u32[]{:S(2)}) %collective-permute-start) | collective-permute-done | bytes 98336 | tf_op jit(solution)/shard_map/ppermute | solution.py:20
  75.0 0.0 copy-start.1
  75.0 8.5 %fusion.6 = f32[128,4096]{1,0:T(8,128)S(1)} fusion(f32[2,128,4096]{2,1,0:T(8,128)} %copy-done.6, f32[2,1,4096]{2,1,0:T(1,128)S(1)} %get-tuple-element.44, f32[2,1,4096]{2,1,0:T(1,128)S(1)} %get-tuple-element.41, f32[2,128,4096]{2,1,0:T(8,128)} %get-tuple-element.18), kind=kLoop, calls=%fused_computation.11 | loop fusion | flops 6815744 | bytes 10551296 | tf_op jit(solution)/shard_map/reduce_sum | solution.py:112
  83.5 1.8 multiply_subtract_fusion.1
  85.3 0.0 all-gather.3.cloned.1.call-update
  85.3 0.0 copy-start.12
  85.3 1.9 convert_element_type.25
  87.3 1.3 copy-done.9
  88.6 1.9 collective-permute-start.5
  90.5 4.5 %collective-permute-start.6 = (f32[1,4096]{1,0:T(1,128)S(1)}, f32[1,4096]{1,0:T(1,128)S(1)}, u32[]{:S(2)}, u32[]{:S(2)}) collective-permute-start(f32[1,4096]{1,0:T(1,128)S(1)} %get-tuple-element.34), channel_id=1, source_target_pairs={{4,0},{8,4},{12,8},{16,12},{20,16},{24,20},{28,24},{5,1},{9,5},{13... | collective-permute-start | bytes 49160 | tf_op jit(solution)/shard_map/ppermute | solution.py:23
  95.1 2.5 convert_element_type.23
  97.6 136.8 %all-gather.3.cloned.1.call-done = f32[512,4096]{1,0:T(8,128)} async-done(((f32[128,4096]{1,0:T(8,128)}), f32[512,4096]{1,0:T(8,128)}) %all-gather.3.cloned.1.call-update) | async-done | bytes 8388624 | tf_op jit(solution)/shard_map/all_gather | solution.py:80
  234.4 5.5 %reduce_sum.19 = f32[128,4096]{1,0:T(8,128)} reduce(f32[4,128,4096]{2,1,0:T(8,128)} %bitcast.26, f32[]{:T(128)} %constant.49.clone.1), dimensions={0}, to_apply=%region_1.2 | reduce | flops 1572864 | bytes 10485764 | tf_op jit(solution)/shard_map/reduce_sum | solution.py:80
  239.9 4.2 %multiply_subtract_fusion = f32[128,4096]{1,0:T(8,128)S(1)} fusion(f32[128,4096]{1,0:T(8,128)} %param.15, f32[128,4096]{1,0:T(8,128)} %reduce_sum.19, f32[128,4096]{1,0:T(8,128)} %param.16, s32[128,4096]{1,0:T(8,128)} %param.17), kind=kLoop, calls=%fused_computation.96 | loop fusion | flops 2621440 | bytes 10485760 | tf_op jit(solution)/shard_map/sub | solution.py:116
  244.2 2.0 collective-permute-start.3
  246.2 4.7 %collective-permute-start.4 = (f32[1,4096]{1,0:T(1,128)S(1)}, f32[1,4096]{1,0:T(1,128)S(1)}, u32[]{:S(2)}, u32[]{:S(2)}) collective-permute-start(f32[1,4096]{1,0:T(1,128)S(1)} %get-tuple-element.36), channel_id=1, source_target_pairs={{4,0},{8,4},{12,8},{16,12},{20,16},{24,20},{28,24},{5,1},{9,5},{13... | collective-permute-start | bytes 49160 | tf_op jit(solution)/shard_map/ppermute | solution.py:23
  250.9 0.7 select_maximum_fusion.6
  251.6 0.5 collective-permute-done.4
  252.1 0.7 select_maximum_fusion.8
  252.8 0.8 fusion.15
  253.6 1.3 fusion.18
  254.9 0.0 copy-start.7
  254.9 1.8 slice_add_fusion.6
  256.7 2.7 collective-permute-start.7
  259.4 3.9 %collective-permute-start.8 = (f32[1,4096]{1,0:T(1,128)S(1)}, f32[1,4096]{1,0:T(1,128)S(1)}, u32[]{:S(2)}, u32[]{:S(2)}) collective-permute-start(f32[1,4096]{1,0:T(1,128)S(1)} %get-tuple-element.32), channel_id=1, source_target_pairs={{4,0},{8,4},{12,8},{16,12},{20,16},{24,20},{28,24},{5,1},{9,5},{13... | collective-permute-start | bytes 49160 | tf_op jit(solution)/shard_map/ppermute | solution.py:23
  263.4 2.4 multiply_add_fusion
  265.8 2.5 convert_element_type.22
  268.3 0.7 select_maximum_fusion.4
  269.0 0.8 fusion.21
  269.8 1.3 fusion.24
  271.1 1.8 slice_add_fusion.4
  272.9 2.4 collective-permute-start.10
  275.3 2.2 collective-permute-start.9
  277.5 0.6 fusion.38
  278.2 3.1 collective-permute-done.9
  281.3 0.7 select_maximum_fusion.2
  282.0 0.8 fusion.27
  282.8 1.3 fusion.30
  284.1 1.9 slice_add_fusion.2
  286.0 1.9 collective-permute-start.11
  287.9 4.5 %collective-permute-start.12 = (f32[1,4096]{1,0:T(1,128)S(1)}, f32[1,4096]{1,0:T(1,128)S(1)}, u32[]{:S(2)}, u32[]{:S(2)}) collective-permute-start(f32[1,4096]{1,0:T(1,128)S(1)} %get-tuple-element.28), channel_id=1, source_target_pairs={{4,0},{8,4},{12,8},{16,12},{20,16},{24,20},{28,24},{5,1},{9,5},{13... | collective-permute-start | bytes 49160 | tf_op jit(solution)/shard_map/ppermute | solution.py:23
  292.5 5.4 %fusion.1 = f32[2,129,4096]{2,1,0:T(8,128)S(1)} fusion(f32[2,128,4096]{2,1,0:T(8,128)S(1)} %copy-done.2, f32[2,1,4096]{2,1,0:T(1,128)S(1)} %get-tuple-element.45, f32[2,1,4096]{2,1,0:T(1,128)S(1)} %get-tuple-element.42, f32[2,1,4096]{2,1,0:T(1,128)S(1)} %get-tuple-element.43, f32[2,128,4096]{2,1,0:T(8,128)} %convert_element_type.22, ...), kind=kLoop, calls=%fused_computation.3 | loop fusion | flops 11624448 | bytes 12746752 | tf_op jit(solution)/shard_map/add | solution.py:41
  297.9 0.7 select_maximum_fusion
  298.6 2.2 fusion.33
  300.8 2.6 fusion.36
  303.4 9.2 %maximum_divide_fusion = (f32[128,4096]{1,0:T(8,128)}, f32[128,4096]{1,0:T(8,128)}) fusion(f32[128,4096]{1,0:T(8,128)} %copy-done.5, f32[128,4096]{1,0:T(8,128)} %param.14, f32[130,4097]{1,0:T(8,128)} %fusion.36, f32[129,4098]{1,0:T(8,128)} %fusion.33, f32[128,4096]{1,0:T(8,128)} %copy-done.4), kind=kLoop, calls=%fused_computation.95 | loop fusion | flops 3670016 | bytes 18874368 | tf_op jit(solution)/shard_map/div | solution.py:126
  312.6 5.4 %fusion.11 = f32[2,128,4096]{2,1,0:T(8,128)} fusion(f32[2,128,4096]{2,1,0:T(8,128)S(1)} %copy-done.2, f32[2,128,4097]{2,1,0:T(8,128)S(1)} %multiply_add_fusion, f32[2,129,4096]{2,1,0:T(8,128)S(1)} %fusion.1, f32[2,128,4096]{2,1,0:T(8,128)S(1)} %fusion.38, f32[128,4096]{1,0:T(8,128)} %get-tuple-element.16, f32[128,4096]{1,0:T(8,128)} %get-tuple-element.14), kind=kLoop, calls=%fused_computation.18 | loop fusion | flops 8388608 | bytes 33554432 | tf_op jit(solution)/shard_map/mul | solution.py:126
  (45 shorter events, 0.4 us)
Async XLA Ops:
  7.2 4.4 %copy-start.8 = (bf16[2,128,4096]{2,1,0:T(8,128)(2,1)S(1)}, bf16[2,128,4096]{2,1,0:T(8,128)(2,1)}, u32[]{:S(2)}) copy-start(bf16[2,128,4096]{2,1,0:T(8,128)(2,1)} %param.11) | copy-start | bytes 6291460
  7.2 227.2 %all-gather.3.cloned.1.call-start = ((), (), s32[]{:S(2)}) async-start(), calls=%async_computation | async-start | bytes 10485760 | tf_op jit(solution)/shard_map/all_gather | solution.py:80
  7.2 4.3 %copy-start = (f32[2,128,4096]{2,1,0:T(8,128)S(1)}, f32[2,128,4096]{2,1,0:T(8,128)}, u32[]{:S(2)}) copy-start(f32[2,128,4096]{2,1,0:T(8,128)} %param.10) | copy-start | bytes 12582916
  7.2 4.7 %copy-start.16 = (f32[128,4096]{1,0:T(8,128)S(1)}, f32[128,4096]{1,0:T(8,128)}, u32[]{:S(2)}) copy-start(f32[128,4096]{1,0:T(8,128)} %param.15) | copy-start | bytes 6291460
  9.9 49.5 %collective-permute-start.2 = (f32[128,4096]{1,0:T(8,128)S(1)}, f32[128,4096]{1,0:T(8,128)S(1)}, u32[]{:S(2)}, u32[]{:S(2)}) collective-permute-start(f32[128,4096]{1,0:T(8,128)S(1)} %get-tuple-element.22), channel_id=1, source_target_pairs={{1,0},{2,1},{3,2},{5,4},{6,5},{7,6},{9,8},{10,9},{11,10},{13,12},{... | collective-permute-start | bytes 6291464 | tf_op jit(solution)/shard_map/ppermute | solution.py:31
  15.2 1.3 copy-start.5
  15.2 44.2 %copy-start.11 = (bf16[2,128,4096]{2,1,0:T(8,128)(2,1)S(1)}, bf16[2,128,4096]{2,1,0:T(8,128)(2,1)}, u32[]{:S(2)}) copy-start(bf16[2,128,4096]{2,1,0:T(8,128)(2,1)} %param.12) | copy-start | bytes 6291460
  15.2 44.2 %copy-start.13 = (f32[128,4096]{1,0:T(8,128)S(1)}, f32[128,4096]{1,0:T(8,128)}, u32[]{:S(2)}) copy-start(f32[128,4096]{1,0:T(8,128)} %param.13) | copy-start | bytes 6291460
  63.8 2.0 copy-start.6
  66.2 4.4 %collective-permute-start.1 = (f32[3,2,1,4096]{3,2,1,0:T(1,128)S(1)}, f32[3,2,1,4096]{3,2,1,0:T(1,128)S(1)}, u32[]{:S(2)}, u32[]{:S(2)}) collective-permute-start(f32[3,2,1,4096]{3,2,1,0:T(1,128)S(1)} %get-tuple-element.39), channel_id=1, source_target_pairs={{4,0},{8,4},{12,8},{16,12},{20,16},{24,20},{28,24},{5,1},{9,5},{13... | collective-permute-start | bytes 294920 | tf_op jit(solution)/shard_map/ppermute | solution.py:23
  68.1 6.8 %collective-permute-start = (f32[3,2,1,4096]{3,2,1,0:T(1,128)S(1)}, f32[3,2,1,4096]{3,2,1,0:T(1,128)S(1)}, u32[]{:S(2)}, u32[]{:S(2)}) collective-permute-start(f32[3,2,1,4096]{3,2,1,0:T(1,128)S(1)} %get-tuple-element.40), channel_id=1, source_target_pairs={{0,4},{4,8},{8,12},{12,16},{16,20},{20,24},{24,28},{1,5},{5,9},{9,... | collective-permute-start | bytes 294920 | tf_op jit(solution)/shard_map/ppermute | solution.py:20
  75.0 8.5 %copy-start.1 = (f32[2,128,4096]{2,1,0:T(8,128)S(1)}, f32[2,128,4096]{2,1,0:T(8,128)}, u32[]{:S(2)}) copy-start(f32[2,128,4096]{2,1,0:T(8,128)} %param.10) | copy-start | bytes 12582916
  75.0 8.5 %copy-start.14 = (f32[128,4096]{1,0:T(8,128)S(1)}, f32[128,4096]{1,0:T(8,128)}, u32[]{:S(2)}) copy-start(f32[128,4096]{1,0:T(8,128)} %param.13) | copy-start | bytes 6291460
  85.3 9.7 %copy-start.12 = (bf16[2,128,4096]{2,1,0:T(8,128)(2,1)S(1)}, bf16[2,128,4096]{2,1,0:T(8,128)(2,1)}, u32[]{:S(2)}) copy-start(bf16[2,128,4096]{2,1,0:T(8,128)(2,1)} %param.12) | copy-start | bytes 6291460
  87.2 1.3 copy-start.9
  88.6 162.3 %collective-permute-start.5 = (f32[1,4096]{1,0:T(1,128)S(1)}, f32[1,4096]{1,0:T(1,128)S(1)}, u32[]{:S(2)}, u32[]{:S(2)}) collective-permute-start(f32[1,4096]{1,0:T(1,128)S(1)} %get-tuple-element.33), channel_id=1, source_target_pairs={{0,4},{4,8},{8,12},{12,16},{16,20},{20,24},{24,28},{1,5},{5,9},{9,... | collective-permute-start | bytes 49160 | tf_op jit(solution)/shard_map/ppermute | solution.py:20
  90.5 160.4 %collective-permute-start.6 = (f32[1,4096]{1,0:T(1,128)S(1)}, f32[1,4096]{1,0:T(1,128)S(1)}, u32[]{:S(2)}, u32[]{:S(2)}) collective-permute-start(f32[1,4096]{1,0:T(1,128)S(1)} %get-tuple-element.34), channel_id=1, source_target_pairs={{4,0},{8,4},{12,8},{16,12},{20,16},{24,20},{28,24},{5,1},{9,5},{13... | collective-permute-start | bytes 49160 | tf_op jit(solution)/shard_map/ppermute | solution.py:23
  239.9 10.9 %copy-start.10 = (f32[128,4096]{1,0:T(8,128)S(1)}, f32[128,4096]{1,0:T(8,128)}, u32[]{:S(2)}) copy-start(f32[128,4096]{1,0:T(8,128)} %copy-done.9) | copy-start | bytes 6291460
  244.2 7.4 %collective-permute-start.3 = (f32[1,4096]{1,0:T(1,128)S(1)}, f32[1,4096]{1,0:T(1,128)S(1)}, u32[]{:S(2)}, u32[]{:S(2)}) collective-permute-start(f32[1,4096]{1,0:T(1,128)S(1)} %get-tuple-element.35), channel_id=1, source_target_pairs={{0,4},{4,8},{8,12},{12,16},{16,20},{20,24},{24,28},{1,5},{5,9},{9,... | collective-permute-start | bytes 49160 | tf_op jit(solution)/shard_map/ppermute | solution.py:20
  246.2 5.9 %collective-permute-start.4 = (f32[1,4096]{1,0:T(1,128)S(1)}, f32[1,4096]{1,0:T(1,128)S(1)}, u32[]{:S(2)}, u32[]{:S(2)}) collective-permute-start(f32[1,4096]{1,0:T(1,128)S(1)} %get-tuple-element.36), channel_id=1, source_target_pairs={{4,0},{8,4},{12,8},{16,12},{20,16},{24,20},{28,24},{5,1},{9,5},{13... | collective-permute-start | bytes 49160 | tf_op jit(solution)/shard_map/ppermute | solution.py:23
  254.9 8.5 %copy-start.2 = (f32[2,128,4096]{2,1,0:T(8,128)S(1)}, f32[2,128,4096]{2,1,0:T(8,128)}, u32[]{:S(2)}) copy-start(f32[2,128,4096]{2,1,0:T(8,128)} %param.10) | copy-start | bytes 12582916
  254.9 8.5 %copy-start.7 = (f32[2,128,4096]{2,1,0:T(8,128)S(1)}, f32[2,128,4096]{2,1,0:T(8,128)}, u32[]{:S(2)}) copy-start(f32[2,128,4096]{2,1,0:T(8,128)} %convert_element_type.23) | copy-start | bytes 12582916
  256.7 11.6 %collective-permute-start.7 = (f32[1,4096]{1,0:T(1,128)S(1)}, f32[1,4096]{1,0:T(1,128)S(1)}, u32[]{:S(2)}, u32[]{:S(2)}) collective-permute-start(f32[1,4096]{1,0:T(1,128)S(1)} %get-tuple-element.31), channel_id=1, source_target_pairs={{0,4},{4,8},{8,12},{12,16},{16,20},{20,24},{24,28},{1,5},{5,9},{9,... | collective-permute-start | bytes 49160 | tf_op jit(solution)/shard_map/ppermute | solution.py:20
  259.4 8.8 %collective-permute-start.8 = (f32[1,4096]{1,0:T(1,128)S(1)}, f32[1,4096]{1,0:T(1,128)S(1)}, u32[]{:S(2)}, u32[]{:S(2)}) collective-permute-start(f32[1,4096]{1,0:T(1,128)S(1)} %get-tuple-element.32), channel_id=1, source_target_pairs={{4,0},{8,4},{12,8},{16,12},{20,16},{24,20},{28,24},{5,1},{9,5},{13... | collective-permute-start | bytes 49160 | tf_op jit(solution)/shard_map/ppermute | solution.py:23
  271.1 6.4 %copy-start.3 = (f32[2,128,4096]{2,1,0:T(8,128)S(1)}, f32[2,128,4096]{2,1,0:T(8,128)}, u32[]{:S(2)}) copy-start(f32[2,128,4096]{2,1,0:T(8,128)} %get-tuple-element.20) | copy-start | bytes 12582916
  271.1 6.4 %copy-start.15 = (f32[128,4096]{1,0:T(8,128)S(1)}, f32[128,4096]{1,0:T(8,128)}, u32[]{:S(2)}) copy-start(f32[128,4096]{1,0:T(8,128)} %param.16) | copy-start | bytes 6291460
  272.9 5.2 %collective-permute-start.10 = (f32[1,4096]{1,0:T(1,128)S(1)}, f32[1,4096]{1,0:T(1,128)S(1)}, u32[]{:S(2)}, u32[]{:S(2)}) collective-permute-start(f32[1,4096]{1,0:T(1,128)S(1)} %get-tuple-element.30), channel_id=1, source_target_pairs={{4,0},{8,4},{12,8},{16,12},{20,16},{24,20},{28,24},{5,1},{9,5},{13... | collective-permute-start | bytes 49160 | tf_op jit(solution)/shard_map/ppermute | solution.py:23
  275.3 6.0 %collective-permute-start.9 = (f32[1,4096]{1,0:T(1,128)S(1)}, f32[1,4096]{1,0:T(1,128)S(1)}, u32[]{:S(2)}, u32[]{:S(2)}) collective-permute-start(f32[1,4096]{1,0:T(1,128)S(1)} %get-tuple-element.29), channel_id=1, source_target_pairs={{0,4},{4,8},{8,12},{12,16},{16,20},{20,24},{24,28},{1,5},{5,9},{9,... | collective-permute-start | bytes 49160 | tf_op jit(solution)/shard_map/ppermute | solution.py:20
  285.9 11.9 %copy-start.4 = (f32[128,4096]{1,0:T(8,128)}, f32[128,4096]{1,0:T(8,128)S(1)}, u32[]{:S(2)}) copy-start(f32[128,4096]{1,0:T(8,128)S(1)} %slice_add_fusion.2) | copy-start | bytes 6291460
  286.0 11.8 %collective-permute-start.11 = (f32[1,4096]{1,0:T(1,128)S(1)}, f32[1,4096]{1,0:T(1,128)S(1)}, u32[]{:S(2)}, u32[]{:S(2)}) collective-permute-start(f32[1,4096]{1,0:T(1,128)S(1)} %get-tuple-element.27), channel_id=1, source_target_pairs={{0,4},{4,8},{8,12},{12,16},{16,20},{20,24},{24,28},{1,5},{5,9},{9,... | collective-permute-start | bytes 49160 | tf_op jit(solution)/shard_map/ppermute | solution.py:20
  287.9 9.9 %collective-permute-start.12 = (f32[1,4096]{1,0:T(1,128)S(1)}, f32[1,4096]{1,0:T(1,128)S(1)}, u32[]{:S(2)}, u32[]{:S(2)}) collective-permute-start(f32[1,4096]{1,0:T(1,128)S(1)} %get-tuple-element.28), channel_id=1, source_target_pairs={{4,0},{8,4},{12,8},{16,12},{20,16},{24,20},{28,24},{5,1},{9,5},{13... | collective-permute-start | bytes 49160 | tf_op jit(solution)/shard_map/ppermute | solution.py:23
Sparse Core Ops, SparseCore 0:
  85.4 148.9 all-gather.2
